TPU v7x, 32 devices: a whole 2x2x4 slice. The times are simulated.
32 devices in a mesh: groups: 2 (over x), chan: 16 (over z, y, core).
Axes of the slice: x: 2, y: 2, z: 4, core: 2. Of those that a mesh axis runs over, the one named last changes fastest.
Arguments:
- voltages: int32 [4096, 79, 2048], P(('groups', 'chan')), parts along dimension 0, may hold values from -96 to 96, as said below
- input_mask: int32 [4096], P(('groups', 'chan')), parts along dimension 0, may hold values 0 or 1
- fir_taps: float32 [16, 2048], replicated, may hold values from -1.5 to 1.5
Outputs:
- visibilities: bfloat16 [32768, 2048], P(('groups', 'chan')), parts along dimension 0
There are 2 independent parts, one for each index of `groups`. A program takes and returns all parts, laid end to end along the dimension named above; an argument that names none is the same for every part. Nothing has to cross between parts.
Inputs may be any that keep to these rules, and one draw needn't show every extreme that they name: `voltages`: 8-bit voltage samples; each input's amplitude, colour and share of a common signal differ.
All inputs are finite; a program needn't handle non-finite values. No bound on the sum of `input_mask` on one device may be relied on, other than what follows from the above.
Results may differ from a plain program's by a relative error of at most 0.006.
Values may be sent and summed in bfloat16 or wider, within the bound.
A program may use at most 320 MiB of HBM per device.

v0:
```python
from functools import reduce
import math
import jax
import jax.numpy as jnp
from jax import lax
from jax.sharding import PartitionSpec as P

INPUTS = 2048
NFFT = 2048
TAPS = 16
SPEC = 64
epsilon = 1e-05


def swapped(value, axis, stride):
    return lax.ppermute(value, axis, [(i, i ^ 1 << stride) for i in range(lax.axis_size(axis))])


def dft_matrix(length, channels):
    column = jnp.arange(length, dtype=jnp.int32)[:, None]
    channel = jnp.arange(1, channels + 1, dtype=jnp.int32)[None, :]
    phases = column * channel % length
    angles = phases.astype(jnp.float32) * (2.0 * math.pi / length)
    return jnp.concatenate([jnp.cos(angles), -jnp.sin(angles)], axis=1).astype(jnp.bfloat16)


def add_terms(left, right):
    return left + right


def polyphase(voltages, input_mask, fir_taps):
    samples = (voltages * input_mask[:, None, None]).astype(jnp.bfloat16)
    terms = [
        fir_taps[offset][None, None, :] * samples[:, offset : offset + SPEC, :]
        for offset in range(TAPS)
    ]
    filtered = reduce(add_terms, terms)
    return filtered.astype(jnp.bfloat16)


def contract(left, right):
    return lax.dot_general(
        left, right, (((1,), (1,)), ((), ())), preferred_element_type=jnp.float32
    )


def on_device(voltages, input_mask, fir_taps):
    devices = lax.axis_size("chan")
    channels = devices // 2
    local_inputs = voltages.shape[0]
    filtered = polyphase(voltages, input_mask, fir_taps)
    spectra = jnp.einsum(
        "isn,nk->iks", filtered, dft_matrix(NFFT, channels), preferred_element_type=jnp.float32
    )
    squares = jnp.sum(spectra * spectra, axis=(0, 2))
    band_partial = squares[:channels] + squares[channels:]
    band_total = lax.psum(band_partial, "chan")
    channel_gain = lax.rsqrt(band_total / (INPUTS * SPEC) + epsilon)
    equalized = (spectra * jnp.concatenate([channel_gain, channel_gain])[None, :, None]).astype(
        jnp.bfloat16
    )
    by_channel = equalized.reshape(local_inputs, 2, channels, SPEC)
    parity = lax.axis_index("chan") % 2
    half_rows = INPUTS // 2
    half_spec = SPEC // 2
    outgoing = by_channel.reshape(local_inputs, 2, channels, 2, half_spec)
    outgoing = outgoing.transpose(2, 3, 0, 1, 4).reshape(devices, local_inputs, SPEC)
    received = lax.all_to_all(outgoing, "chan", split_axis=0, concat_axis=1, tiled=True)[0]
    real_part = received[:, :half_spec]
    imag_part = received[:, half_spec:]
    rotated = jnp.concatenate([imag_part, -real_part], axis=1)
    real_vis = contract(received, received)
    imag_vis = contract(rotated, received)
    row_index = jnp.arange(INPUTS, dtype=jnp.int32)[:, None]
    column_index = jnp.arange(INPUTS, dtype=jnp.int32)[None, :]
    packed = jnp.where(column_index <= row_index, real_vis, imag_vis)
    partner_rows = lax.dynamic_slice_in_dim(packed, (1 - parity) * half_rows, half_rows, 0)
    own_rows = lax.dynamic_slice_in_dim(packed, parity * half_rows, half_rows, 0)
    summed = own_rows + swapped(partner_rows, "chan", 0)
    return (summed / SPEC).astype(jnp.bfloat16)


def solution(mesh):
    return jax.shard_map(
        on_device,
        mesh=mesh,
        in_specs=(P(("groups", "chan"), None, None), P(("groups", "chan")), P()),
        out_specs=P(("groups", "chan"), None),
        check_vma=False,
    )
```

profile of v0, /device:TPU:0, one launch (start us, length us, event | category | flops | bytes accessed | tf_op | source)
XLA Modules:
  0.0 349.4 jit_solution(1774210906190760884)
XLA Ops:
  0.0 1.9 fusion.17
  1.9 1.0 cosine_convert_fusion
  2.8 40.1 %multiply_convert_fusion = bf16[128,79,2048]{2,0,1:T(8,128)(2,1)} fusion(s32[128,79,2048]{2,0,1:T(8,128)} %param.3, s32[128]{0:T(128)} %param.4), kind=kLoop, calls=%fused_computation | loop fusion | flops 41418752 | bytes 124256768 | tf_op jit(solution)/shard_map/convert_element_type | solution.py:32
  42.9 0.0 copy-start
  43.0 0.0 copy-start.1
  43.0 200.1 %add_convert_fusion.1.clone.5 = bf16[128,64,2048]{2,0,1:T(8,128)(2,1)} fusion(bf16[128,79,2048]{2,0,1:T(8,128)(2,1)} %multiply_convert_fusion, f32[2048]{0:T(1024)S(1)} %bitcast.59, f32[2048]{0:T(1024)S(1)} %bitcast.60, f32[2048]{0:T(1024)S(1)} %bitcast.46, f32[2048]{0:T(1024)S(1)} %bitcast.47, f32[2048]{0:T(1024)S(1)} %bitcast.48, ...), kind=kLoop, calls=%fused_computation.1.clone.clone.clone.clone.2 | loop fusion | flops 805306368 | bytes 570556416 | tf_op jit(solution)/shard_map/reduce_sum | solution.py:55
  243.1 0.0 copy-done
  243.1 0.0 copy-done.1
  243.1 14.6 %multiply_reduce_fusion = (f32[16]{0:T(128)S(1)}, f32[16,128,64]{1,0,2:T(8,128)S(1)}) fusion(bf16[2048,8]{0,1:T(8,128)(2,1)S(1)} %copy-done.1, bf16[2048,8]{0,1:T(8,128)(2,1)S(1)} %copy-done, bf16[128,64,2048]{2,0,1:T(8,128)(2,1)} %add_convert_fusion.1.clone.5), kind=kOutput, calls=%fused_computation.7 | convolution fusion | flops 537264128 | bytes 34144320 | tf_op jit(solution)/shard_map/isn,nk->iks/dot_general | solution.py:52
  257.7 0.1 slice_add_fusion
  257.8 34.9 %psum.7 = f32[8]{0:T(128)S(1)} all-reduce(f32[8]{0:T(128)S(1)} %slice_add_fusion), channel_id=1, replica_groups=mesh['groups'=2,'chan'=16] {'chan'}, use_global_device_ids=true, to_apply=%region_1.2 | all-reduce | flops 8 | bytes 64 | tf_op jit(solution)/shard_map/psum | solution.py:57
  292.7 0.1 pad_maximum_fusion
  292.8 0.1 multiply_convert_fusion.2
  292.9 0.8 copy.5
  293.7 3.7 %all-to-all-start = ((bf16[16,128,64]{1,2,0:T(8,128)(2,1)}), bf16[16,128,64]{1,2,0:T(8,128)(2,1)S(1)}, u32[]{:S(2)}, u32[]{:S(2)}) async-start(bf16[16,128,64]{1,2,0:T(8,128)(2,1)} %bitcast.20), calls=%async_computation | async-start | bytes 524288 | tf_op jit(solution)/shard_map/all_to_all | solution.py:68
  297.4 9.8 %all-to-all-done = bf16[16,128,64]{1,2,0:T(8,128)(2,1)S(1)} async-done(((bf16[16,128,64]{1,2,0:T(8,128)(2,1)}), bf16[16,128,64]{1,2,0:T(8,128)(2,1)S(1)}, u32[]{:S(2)}, u32[]{:S(2)}) %all-to-all-start) | async-done | bytes 262176 | tf_op jit(solution)/shard_map/all_to_all | solution.py:68
  307.3 2.4 fusion.15
  309.7 8.6 %fusion.1 = f32[2048,2048]{1,0:T(8,128)} fusion(f32[2048,2048]{1,0:T(8,128)S(1)} %fusion.15, bf16[2048,32]{0,1:T(8,128)(2,1)S(1)} %get-tuple-element.6, bf16[2048,32]{0,1:T(8,128)(2,1)S(1)} %get-tuple-element.5, bf16[16,128,64]{1,2,0:T(8,128)(2,1)S(1)} %all-to-all-done), kind=kOutput, calls=%fused_computation.4 | convolution fusion | flops 545783808 | bytes 34078720 | tf_op jit(solution)/shard_map/dot_general | solution.py:42
  318.3 7.7 %constant_dynamic-slice_fusion = f32[1024,2048]{1,0:T(8,128)} fusion(f32[2048,2048]{1,0:T(8,128)} %fusion.1, s32[]{:T(128)S(6)} %select_n.29), kind=kLoop, calls=%fused_computation.30 | loop fusion | bytes 16777220 | tf_op jit(solution)/shard_map/dynamic_slice | solution.py:77
  326.0 0.0 collective-permute-start
  326.0 13.5 %collective-permute-done = f32[1024,2048]{1,0:T(8,128)} collective-permute-done((f32[1024,2048]{1,0:T(8,128)}, f32[1024,2048]{1,0:T(8,128)}, u32[]{:S(2)}, u32[]{:S(2)}) %collective-permute-start) | collective-permute-done | bytes 8388640 | tf_op jit(solution)/shard_map/ppermute | solution.py:16
  339.5 10.0 %multiply_convert_fusion.1 = bf16[1024,2048]{1,0:T(8,128)(2,1)} fusion(f32[1024,2048]{1,0:T(8,128)} %collective-permute-done, f32[2048,2048]{1,0:T(8,128)} %fusion.1, s32[]{:T(128)S(6)} %select_n.28), kind=kLoop, calls=%fused_computation.5 | loop fusion | flops 6291456 | bytes 20971524 | tf_op jit(solution)/shard_map/convert_element_type | solution.py:80
  (4 shorter events, 0.1 us)
Async XLA Ops:
  42.9 200.1 %copy-start = (bf16[2048,8]{0,1:T(8,128)(2,1)S(1)}, bf16[2048,8]{0,1:T(8,128)(2,1)}, u32[]{:S(2)}) copy-start(bf16[2048,8]{0,1:T(8,128)(2,1)} %get-tuple-element.23) | copy-start | bytes 98308
  43.0 200.1 %copy-start.1 = (bf16[2048,8]{0,1:T(8,128)(2,1)S(1)}, bf16[2048,8]{0,1:T(8,128)(2,1)}, u32[]{:S(2)}) copy-start(bf16[2048,8]{0,1:T(8,128)(2,1)} %get-tuple-element.24) | copy-start | bytes 98308
  293.7 13.5 %all-to-all-start = ((bf16[16,128,64]{1,2,0:T(8,128)(2,1)}), bf16[16,128,64]{1,2,0:T(8,128)(2,1)S(1)}, u32[]{:S(2)}, u32[]{:S(2)}) async-start(bf16[16,128,64]{1,2,0:T(8,128)(2,1)} %bitcast.20), calls=%async_computation | async-start | bytes 524288 | tf_op jit(solution)/shard_map/all_to_all | solution.py:68
  326.0 13.5 %collective-permute-start = (f32[1024,2048]{1,0:T(8,128)}, f32[1024,2048]{1,0:T(8,128)}, u32[]{:S(2)}, u32[]{:S(2)}) collective-permute-start(f32[1024,2048]{1,0:T(8,128)} %constant_dynamic-slice_fusion), channel_id=1, source_target_pairs={{0,1},{1,0},{2,3},{3,2},{4,5},{5,4},{6,7},{7,6},{8,9},{9,8},{10,11... | collective-permute-start | bytes 25165832 | tf_op jit(solution)/shard_map/ppermute | solution.py:16
where the time goes:
time: 350 us; the launch traced here: 349 us
  other arithmetic  251 us (72%)
  blocking collectives  34.9 us (10%)
  matrix products  25.6 us (7%)
  waiting for transfers between devices  23.3 us (7%)
  local copies, waits for them, and re-layouts  10.4 us (3%)
  starting transfers between devices  3.72 us (1%)
    reduce_sum x1, other arithmetic, on_device(): squares = jnp.sum(spectra * spectra, axis=(0, 2))  200 us
    convert_element_type x1, other arithmetic, polyphase(): samples = (voltages * input_mask[:, None, None]).astype(jnp.bfloat16)  40.1 us
    psum x1, blocking collectives, on_device(): band_total = lax.psum(band_partial, 'chan')  34.9 us
    dot_general x1, matrix products, on_device(): jnp.einsum('isn,nk->iks', filtered, dft_matrix(NFFT, channels), preferred...  14.6 us
    ppermute x1, waiting for transfers between devices, swapped(): lax.ppermute(value, axis, [(i, i ^ 1 << stride) for i in range(lax.axis_s...  13.5 us
    dot_general x2, matrix products, contract(): lax.dot_general(left, right, (((1,), (1,)), ((), ())), preferred_element_...  10.9 us
    convert_element_type x1, other arithmetic, on_device(): return (summed / SPEC).astype(jnp.bfloat16)  9.98 us
    all_to_all x1, waiting for transfers between devices, on_device(): lax.all_to_all(outgoing, 'chan', split_axis=0, concat_axis=1, tiled=True)[0]  9.81 us
  transfers between devices with their start and end apart: 2, of which 2 were waited for; matrix products, arithmetic and copies ran while one was open for 0% of the time, Pallas kernels for 0%

commit v1 on v0

--- a/solution.py
+++ b/solution.py
@@ -54,7 +54,11 @@
     )
     squares = jnp.sum(spectra * spectra, axis=(0, 2))
     band_partial = squares[:channels] + squares[channels:]
-    band_total = lax.psum(band_partial, "chan")
+    band_total = band_partial
+    for hop in (1, 2, 4, 8):
+        band_total = band_total + lax.ppermute(
+            band_total, "chan", [(dev, dev ^ hop) for dev in range(16)]
+        )
     channel_gain = lax.rsqrt(band_total / (INPUTS * SPEC) + epsilon)
     equalized = (spectra * jnp.concatenate([channel_gain, channel_gain])[None, :, None]).astype(
         jnp.bfloat16

time: 350 us -> 331 us (0.946)
  blocking collectives: 34.9 us -> 0 us
  starting transfers between devices: 3.72 us -> 14.7 us
  waiting for transfers between devices: 23.3 us -> 28.9 us
    psum x1 -> x0, blocking collectives: 34.9 us -> none  [on_device(): band_total = lax.psum(band_partial, 'chan')]
    ppermute x0 -> x4, starting transfers between devices: none -> 8.39 us  [on_device(): lax.ppermute(band_total, 'chan', [(dev, dev ^ hop) for dev in range(16)])]
    ppermute x0 -> x4, waiting for transfers between devices: none -> 5.37 us  [on_device(): lax.ppermute(band_total, 'chan', [(dev, dev ^ hop) for dev in range(16)])]
  transfers between devices with their start and end apart: 2 -> 6, of which waited for: 2 -> 6; matrix products, arithmetic and copies ran while one was open for 0% -> 0% of each run, Pallas kernels for 0% -> 0%
where the time goes in v1:
time: 331 us
  other arithmetic  251 us (76%)
  waiting for transfers between devices  28.9 us (9%)
  matrix products  25.6 us (8%)
  starting transfers between devices  14.7 us (4%)
  local copies, waits for them, and re-layouts  10.4 us (3%)
    reduce_sum x1, other arithmetic, on_device(): squares = jnp.sum(spectra * spectra, axis=(0, 2))  200 us
    convert_element_type x1, other arithmetic, polyphase(): samples = (voltages * input_mask[:, None, None]).astype(jnp.bfloat16)  40.1 us
    dot_general x1, matrix products, on_device(): jnp.einsum('isn,nk->iks', filtered, dft_matrix(NFFT, channels), preferred...  14.6 us
    ppermute x1, waiting for transfers between devices, swapped(): lax.ppermute(value, axis, [(i, i ^ 1 << stride) for i in range(lax.axis_s...  13.5 us
    dot_general x2, matrix products, contract(): lax.dot_general(left, right, (((1,), (1,)), ((), ())), preferred_element_...  10.9 us
    all_to_all x1, waiting for transfers between devices, on_device(): lax.all_to_all(outgoing, 'chan', split_axis=0, concat_axis=1, tiled=True)[0]  10 us
    convert_element_type x1, other arithmetic, on_device(): return (summed / SPEC).astype(jnp.bfloat16)  9.98 us
    ppermute x4, starting transfers between devices, on_device(): lax.ppermute(band_total, 'chan', [(dev, dev ^ hop) for dev in range(16)])  8.39 us
  transfers between devices with their start and end apart: 6, of which 6 were waited for; matrix products, arithmetic and copies ran while one was open for 0% of the time, Pallas kernels for 0%

profile of v1, /device:TPU:0, one launch (start us, length us, event | category | flops | bytes accessed | tf_op | source)
XLA Modules:
  0.0 330.7 jit_solution(11556437884917384893)
XLA Ops:
  0.0 1.9 fusion.17
  1.9 1.0 cosine_convert_fusion
  2.8 40.1 %multiply_convert_fusion = bf16[128,79,2048]{2,0,1:T(8,128)(2,1)} fusion(s32[128,79,2048]{2,0,1:T(8,128)} %param.3, s32[128]{0:T(128)} %param.4), kind=kLoop, calls=%fused_computation | loop fusion | flops 41418752 | bytes 124256768 | tf_op jit(solution)/shard_map/convert_element_type | solution.py:32
  43.0 0.0 copy-start
  43.0 0.0 copy-start.1
  43.0 199.6 %add_convert_fusion.1.clone.5 = bf16[128,64,2048]{2,0,1:T(8,128)(2,1)} fusion(bf16[128,79,2048]{2,0,1:T(8,128)(2,1)} %multiply_convert_fusion, f32[2048]{0:T(1024)S(1)} %bitcast.59, f32[2048]{0:T(1024)S(1)} %bitcast.60, f32[2048]{0:T(1024)S(1)} %bitcast.46, f32[2048]{0:T(1024)S(1)} %bitcast.47, f32[2048]{0:T(1024)S(1)} %bitcast.48, ...), kind=kLoop, calls=%fused_computation.1.clone.clone.clone.clone.2 | loop fusion | flops 805306368 | bytes 570556416 | tf_op jit(solution)/shard_map/reduce_sum | solution.py:55
  242.6 0.0 copy-done
  242.6 0.0 copy-done.1
  242.6 14.6 %multiply_reduce_fusion = (f32[16]{0:T(128)S(1)}, f32[16,128,64]{1,0,2:T(8,128)S(1)}) fusion(bf16[2048,8]{0,1:T(8,128)(2,1)S(1)} %copy-done.1, bf16[2048,8]{0,1:T(8,128)(2,1)S(1)} %copy-done, bf16[128,64,2048]{2,0,1:T(8,128)(2,1)} %add_convert_fusion.1.clone.5), kind=kOutput, calls=%fused_computation.7 | convolution fusion | flops 537264128 | bytes 34144320 | tf_op jit(solution)/shard_map/isn,nk->iks/dot_general | solution.py:52
  257.3 0.1 slice_add_fusion
  257.3 0.5 collective-permute-start
  257.8 0.8 collective-permute-done
  258.6 0.1 fusion.18
  258.7 2.8 collective-permute-start.1
  261.5 1.5 collective-permute-done.1
  263.0 2.1 collective-permute-start.2
  265.1 1.5 collective-permute-done.2
  266.6 3.0 collective-permute-start.3
  269.7 1.5 collective-permute-done.3
  271.2 0.1 pad_maximum_fusion
  271.3 0.1 multiply_convert_fusion.2
  271.4 0.8 copy.5
  272.2 6.3 %all-to-all-start = ((bf16[16,128,64]{1,2,0:T(8,128)(2,1)}), bf16[16,128,64]{1,2,0:T(8,128)(2,1)S(1)}, u32[]{:S(2)}, u32[]{:S(2)}) async-start(bf16[16,128,64]{1,2,0:T(8,128)(2,1)} %bitcast.20), calls=%async_computation | async-start | bytes 524288 | tf_op jit(solution)/shard_map/all_to_all | solution.py:72
  278.5 10.0 %all-to-all-done = bf16[16,128,64]{1,2,0:T(8,128)(2,1)S(1)} async-done(((bf16[16,128,64]{1,2,0:T(8,128)(2,1)}), bf16[16,128,64]{1,2,0:T(8,128)(2,1)S(1)}, u32[]{:S(2)}, u32[]{:S(2)}) %all-to-all-start) | async-done | bytes 262176 | tf_op jit(solution)/shard_map/all_to_all | solution.py:72
  288.6 2.4 fusion.15
  290.9 8.6 %fusion.1 = f32[2048,2048]{1,0:T(8,128)} fusion(f32[2048,2048]{1,0:T(8,128)S(1)} %fusion.15, bf16[2048,32]{0,1:T(8,128)(2,1)S(1)} %get-tuple-element.6, bf16[2048,32]{0,1:T(8,128)(2,1)S(1)} %get-tuple-element.5, bf16[16,128,64]{1,2,0:T(8,128)(2,1)S(1)} %all-to-all-done), kind=kOutput, calls=%fused_computation.4 | convolution fusion | flops 545783808 | bytes 34078720 | tf_op jit(solution)/shard_map/dot_general | solution.py:42
  299.5 7.7 %constant_dynamic-slice_fusion = f32[1024,2048]{1,0:T(8,128)} fusion(f32[2048,2048]{1,0:T(8,128)} %fusion.1, s32[]{:T(128)S(6)} %select_n.29), kind=kLoop, calls=%fused_computation.30 | loop fusion | bytes 16777220 | tf_op jit(solution)/shard_map/dynamic_slice | solution.py:81
  307.2 0.0 collective-permute-start.4
  307.2 13.5 %collective-permute-done.4 = f32[1024,2048]{1,0:T(8,128)} collective-permute-done((f32[1024,2048]{1,0:T(8,128)}, f32[1024,2048]{1,0:T(8,128)}, u32[]{:S(2)}, u32[]{:S(2)}) %collective-permute-start.4) | collective-permute-done | bytes 8388640 | tf_op jit(solution)/shard_map/ppermute | solution.py:16
  320.7 10.0 %multiply_convert_fusion.1 = bf16[1024,2048]{1,0:T(8,128)(2,1)} fusion(f32[1024,2048]{1,0:T(8,128)} %collective-permute-done.4, f32[2048,2048]{1,0:T(8,128)} %fusion.1, s32[]{:T(128)S(6)} %select_n.28), kind=kLoop, calls=%fused_computation.5 | loop fusion | flops 6291456 | bytes 20971524 | tf_op jit(solution)/shard_map/convert_element_type | solution.py:84
  (6 shorter events, 0.1 us)
Async XLA Ops:
  43.0 199.6 %copy-start = (bf16[2048,8]{0,1:T(8,128)(2,1)S(1)}, bf16[2048,8]{0,1:T(8,128)(2,1)}, u32[]{:S(2)}) copy-start(bf16[2048,8]{0,1:T(8,128)(2,1)} %get-tuple-element.23) | copy-start | bytes 98308
  43.0 199.6 %copy-start.1 = (bf16[2048,8]{0,1:T(8,128)(2,1)S(1)}, bf16[2048,8]{0,1:T(8,128)(2,1)}, u32[]{:S(2)}) copy-start(bf16[2048,8]{0,1:T(8,128)(2,1)} %get-tuple-element.24) | copy-start | bytes 98308
  257.3 1.3 collective-permute-start
  258.7 4.3 %collective-permute-start.1 = (f32[8]{0:T(128)S(1)}, f32[8]{0:T(128)S(1)}, u32[]{:S(2)}, u32[]{:S(2)}) collective-permute-start(f32[8]{0:T(128)S(1)} %fusion.18), channel_id=1, source_target_pairs={{0,2},{1,3},{2,0},{3,1},{4,6},{5,7},{6,4},{7,5},{8,10},{9,11},{10,... | collective-permute-start | bytes 104 | tf_op jit(solution)/shard_map/ppermute | solution.py:59
  263.0 3.6 %collective-permute-start.2 = (f32[8]{0:T(128)S(1)}, f32[8]{0:T(128)S(1)}, u32[]{:S(2)}, u32[]{:S(2)}) collective-permute-start(f32[8]{0:T(128)S(1)} %add.112), channel_id=1, source_target_pairs={{0,4},{1,5},{2,6},{3,7},{4,0},{5,1},{6,2},{7,3},{8,12},{9,13},{10,... | collective-permute-start | bytes 104 | tf_op jit(solution)/shard_map/ppermute | solution.py:59
  266.6 4.6 %collective-permute-start.3 = (f32[8]{0:T(128)S(1)}, f32[8]{0:T(128)S(1)}, u32[]{:S(2)}, u32[]{:S(2)}) collective-permute-start(f32[8]{0:T(128)S(1)} %add.113), channel_id=1, source_target_pairs={{0,8},{1,9},{2,10},{3,11},{4,12},{5,13},{6,14},{7,15},{8,0},{9,1},... | collective-permute-start | bytes 104 | tf_op jit(solution)/shard_map/ppermute | solution.py:59
  272.2 16.3 %all-to-all-start = ((bf16[16,128,64]{1,2,0:T(8,128)(2,1)}), bf16[16,128,64]{1,2,0:T(8,128)(2,1)S(1)}, u32[]{:S(2)}, u32[]{:S(2)}) async-start(bf16[16,128,64]{1,2,0:T(8,128)(2,1)} %bitcast.20), calls=%async_computation | async-start | bytes 524288 | tf_op jit(solution)/shard_map/all_to_all | solution.py:72
  307.2 13.5 %collective-permute-start.4 = (f32[1024,2048]{1,0:T(8,128)}, f32[1024,2048]{1,0:T(8,128)}, u32[]{:S(2)}, u32[]{:S(2)}) collective-permute-start(f32[1024,2048]{1,0:T(8,128)} %constant_dynamic-slice_fusion), channel_id=1, source_target_pairs={{0,1},{1,0},{2,3},{3,2},{4,5},{5,4},{6,7},{7,6},{8,9},{9,8},{10,11... | collective-permute-start | bytes 25165832 | tf_op jit(solution)/shard_map/ppermute | solution.py:16
